TPU v7x, 32 devices: a whole 2x2x4 slice. The times are simulated.
32 devices in a mesh: group: 2 (over y), store: 8 (over z, x), sketch: 2 (over core).
Axes of the slice: x: 2, y: 2, z: 4, core: 2. Of those that a mesh axis runs over, the one named last changes fastest.
Arguments:
- acts: bfloat16 [2, 2048, 4096], P('sketch', ('group', 'store')), parts along dimension 1, may hold values from -6 to 6
- grads: bfloat16 [2, 2048, 4096], P('sketch', ('group', 'store')), parts along dimension 1, may hold values from -6 to 6
- proj_in: bfloat16 [2, 4096, 64], P('sketch'), may hold values from -0.09375 to 0.09375
- proj_out: bfloat16 [2, 4096, 64], P('sketch'), may hold values from -0.09375 to 0.09375
- token_ids: int32 [2048], P(('group', 'store')), parts along dimension 0, may hold values from 0 to 128004, as said below
- store: bfloat16 [3072, 8192], P(('group', 'store'), 'sketch'), parts along dimension 0, may hold values from -0.59765625 to 0.59765625
- row_example: int32 [3072], P(('group', 'store')), parts along dimension 0, may hold values from 0 to 95
Outputs:
- example_scores: float32 [192, 8], P(('group', 'store', 'sketch')), parts along dimension 0
There are 2 independent parts, one for each index of `group`. A program takes and returns all parts, laid end to end along the dimension named above; an argument that names none is the same for every part. Nothing has to cross between parts.
Inputs may be any that keep to these rules, and one draw needn't show every extreme that they name: `token_ids`: each query's 128 slots hold ids below 128000 in a first run of at least 64 slots and the padding id 128004 after it; some query has no padding.
All inputs are finite; a program needn't handle non-finite values.
Results may differ from a plain program's by a relative error of at most 0.003.
Values may be sent and summed in bfloat16 or wider, within the bound.
A program may use at most 64 MiB of HBM per device.

v0:
```python
import jax
import jax.numpy as jnp
from jax import lax
from jax.sharding import PartitionSpec as P

SEQ = 128


def example_term(row_example, values, count):
    labels = lax.broadcasted_iota(jnp.int32, (1, count), 1)
    onehot = (row_example[:, None] == labels).astype(jnp.float32)
    return lax.dot_general(
        onehot,
        values,
        (((0,), (0,)), ((), ())),
        precision=lax.Precision.HIGHEST,
        preferred_element_type=jnp.float32,
    )


def local(acts, grads, proj_in, proj_out, token_ids, store, row_example):
    width = proj_in.shape[2]
    queries_here = acts.shape[1] // SEQ
    keep = (token_ids != 128004).astype(jnp.float32).reshape(queries_here, SEQ)
    count = jnp.sum(keep, axis=1)
    xp = jnp.dot(acts[0], proj_in[0], preferred_element_type=jnp.float32).reshape(
        queries_here, SEQ, width
    )
    gp = jnp.dot(grads[0], proj_out[0], preferred_element_type=jnp.float32).reshape(
        queries_here, SEQ, width
    )
    outer = jnp.einsum("qsk,qsj->qkj", gp * keep[:, :, None], xp, precision=lax.Precision.HIGHEST)
    pieces = (outer / count[:, None, None]).reshape(queries_here, width * width)
    sketch = pieces.astype(jnp.bfloat16)
    scores = lax.dot_general(
        store,
        lax.all_gather(sketch, "store", axis=0, tiled=True),
        (((1,), (1,)), ((), ())),
        preferred_element_type=jnp.float32,
    )
    n_cores = lax.axis_size("sketch")
    share = row_example.shape[0] // (16 * n_cores)
    result = lax.psum_scatter(
        example_term(row_example, scores, share * lax.axis_size(("store", "sketch"))),
        ("store", "sketch"),
        scatter_dimension=0,
        tiled=True,
    )
    return result


def solution(mesh):
    in_specs = (
        P("sketch", ("group", "store"), None),
        P("sketch", ("group", "store"), None),
        P("sketch", None, None),
        P("sketch", None, None),
        P(("group", "store")),
        P(("group", "store"), "sketch"),
        P(("group", "store")),
    )
    out_specs = P(("group", "store", "sketch"), None)
    return jax.shard_map(local, mesh=mesh, in_specs=in_specs, out_specs=out_specs, check_vma=False)
```

profile of v0, /device:TPU:0, one launch (start us, length us, event | category | flops | bytes accessed | tf_op | source)
XLA Modules:
  0.0 97.5 jit_solution(13876375183453694045)
XLA Ops:
  0.0 0.0 copy-start
  0.0 0.0 copy-start.1
  0.0 0.0 copy-start.2
  0.0 0.8 compare_convert_fusion
  0.8 0.0 copy-start.4
  0.8 1.9 %convolution_multiply_fusion = f32[128,64]{0,1:T(8,128)S(1)} fusion(bf16[1,128,4096]{2,1,0:T(8,128)(2,1)} %param.8, bf16[1,4096,64]{1,2,0:T(8,128)(2,1)} %param.10, f32[128]{0:T(128)S(1)} %compare_convert_fusion), kind=kOutput, calls=%fused_computation.1 | convolution fusion | flops 67117056 | bytes 1606144 | tf_op jit(solution)/shard_map/dot_general | solution.py:29
  2.7 0.0 copy-done.1
  2.7 0.0 copy-done.2
  2.7 0.0 copy-start.3
  2.8 0.0 copy-start.5
  2.8 0.5 fusion.1
  3.3 0.0 copy-done.4
  3.3 0.6 fusion.13
  3.9 0.8 fusion
  4.7 0.1 reshape.34
  4.8 32.3 %all-gather = bf16[8,1,4096]{2,1,0:T(2,128)(2,1)S(1)} all-gather(bf16[1,1,4096]{2,1,0:T(2,128)(2,1)S(1)} %reshape.34), channel_id=1, replica_groups=mesh['group'=2,'store'=8,'sketch'=2] {'store'}, dimensions={0}, use_global_device_ids=true | all-gather | bytes 73728 | tf_op jit(solution)/shard_map/all_gather | solution.py:37
  37.1 0.0 copy-done
  37.1 0.5 fusion.7
  37.6 0.0 copy-done.3
  37.6 0.3 fusion.10
  37.9 57.7 %all-reduce = f32[96,8]{1,0:T(8,128)S(1)} all-reduce(f32[96,8]{1,0:T(8,128)S(1)} %fusion.10), channel_id=2, replica_groups=mesh['group'=2,'store'=8,'sketch'=2] {'store','sketch'}, use_global_device_ids=true, to_apply=%region_1.0.clone | all-reduce | flops 768 | bytes 6144
  95.7 0.0 copy-done.5
  95.7 0.6 dynamic-slice
  96.9 0.6 constant_dynamic-slice_fusion
Async XLA Ops:
  0.0 37.1 %copy-start = (bf16[192,4096]{1,0:T(8,128)(2,1)S(1)}, bf16[192,4096]{1,0:T(8,128)(2,1)}, u32[]{:S(2)}) copy-start(bf16[192,4096]{1,0:T(8,128)(2,1)} %param.12) | copy-start | bytes 4718596
  0.0 2.7 %copy-start.1 = (bf16[1,128,4096]{2,1,0:T(8,128)(2,1)S(1)}, bf16[1,128,4096]{2,1,0:T(8,128)(2,1)}, u32[]{:S(2)}) copy-start(bf16[1,128,4096]{2,1,0:T(8,128)(2,1)} %param.7) | copy-start | bytes 3145732
  0.0 2.7 %copy-start.2 = (bf16[1,4096,64]{1,2,0:T(8,128)(2,1)S(1)}, bf16[1,4096,64]{1,2,0:T(8,128)(2,1)}, u32[]{:S(2)}) copy-start(bf16[1,4096,64]{1,2,0:T(8,128)(2,1)} %param.9) | copy-start | bytes 1572868
  0.8 2.4 %copy-start.4 = (s32[128]{0:T(128)S(1)}, s32[128]{0:T(128)}, u32[]{:S(2)}) copy-start(s32[128]{0:T(128)} %param.11) | copy-start | bytes 1540
  2.7 34.9 %copy-start.3 = (s32[192]{0:T(256)S(1)}, s32[192]{0:T(256)}, u32[]{:S(2)}) copy-start(s32[192]{0:T(256)} %param.13) | copy-start | bytes 2308
  2.8 92.9 %copy-start.5 = (u32[32]{0:T(128)S(1)}, u32[32]{0:T(128)}, u32[]{:S(2)}) copy-start(u32[32]{0:T(128)} %constant.10) | copy-start | bytes 388
where the time goes:
time: 97.7 us; the launch traced here: 97.5 us
  blocking collectives  90 us (92%)
  matrix products  4.05 us (4%)
  other arithmetic  1.41 us (1%)
  local copies, waits for them, and re-layouts  1.3 us (1%)
    unnamed x1, blocking collectives  57.7 us
    all_gather x1, blocking collectives, local(): lax.all_gather(sketch, 'store', axis=0, tiled=True)  32.3 us

commit v1 on v0

v1 whole, which is shorter than its diff:
```python
import functools

import jax
import jax.numpy as jnp
from jax import lax
from jax.experimental import pallas as pl
from jax.experimental.pallas import tpu as pltpu
from jax.sharding import PartitionSpec as P

SEQ = 128
PAD_ID = 128004
LANES = 128
SUBLANES = 8
NT = (((1,), (1,)), ((), ()))
MESH = pl.DeviceIdType.MESH


def each(start, stop, body):
    if stop - start <= 16:
        for i in range(start, stop):
            body(i)
    else:
        lax.fori_loop(start, stop, lambda i, carry: (body(i), carry)[1], 0)


def split(value):
    high = value.astype(jnp.bfloat16)
    return high, (value - high.astype(jnp.float32)).astype(jnp.bfloat16)


def kernel(
    n_store, n_sketch, share,
    acts_hbm, grads_hbm, pin_hbm, pout_hbm, ids_ref, store_hbm, rows_ref,
    out_ref,
    acts, grads, pin, pout, store, outer_ref, mine, sketches, wide, sums_hi, sums_lo, parts, landed,
    load_sem, s_send, s_recv, p_send, p_recv,
):
    loads = [
        pltpu.make_async_copy(src, dst, load_sem.at[i])
        for i, (src, dst) in enumerate(
            ((pout_hbm, pout), (grads_hbm, grads), (pin_hbm, pin), (acts_hbm, acts), (store_hbm, store))
        )
    ]
    for load in loads:
        load.start()

    here = lax.axis_index("store")
    core = lax.axis_index("sketch")
    n_all = n_store * n_sketch
    me = here * n_sketch + core

    def peer(step):
        to = lax.rem(me + step, n_all)
        return {"store": to // n_sketch, "sketch": lax.rem(to, n_sketch)}

    barrier = pltpu.get_barrier_semaphore()
    each(1, n_all, lambda i: pl.semaphore_signal(barrier, 1, device_id=peer(i), device_id_type=MESH))

    width = pout.shape[0]
    keep = (ids_ref[...] != PAD_ID).astype(jnp.float32)
    count = jnp.sum(keep, axis=1, keepdims=True)
    loads[0].wait()
    loads[1].wait()
    gp = lax.dot_general(pout[...], grads[...], NT, preferred_element_type=jnp.float32) * keep
    loads[2].wait()
    loads[3].wait()
    xp = lax.dot_general(pin[...], acts[...], NT, preferred_element_type=jnp.float32)
    g_hi, g_lo = split(gp)
    x_hi, x_lo = split(xp)
    outer_ref[...] = lax.dot_general(
        jnp.concatenate([g_hi, g_lo, g_hi], axis=1),
        jnp.concatenate([x_hi, x_hi, x_lo], axis=1),
        NT,
        preferred_element_type=jnp.float32,
    )
    half = width // 2
    flat = jnp.concatenate(
        [outer_ref[pl.ds(0, half, stride=2), :], outer_ref[pl.ds(1, half, stride=2), :]], axis=1
    )
    sketch = (flat / count).astype(jnp.bfloat16)
    mine[...] = sketch
    sketches[here] = sketch

    pl.semaphore_wait(barrier, n_all - 1)

    def sketch_copy(step):
        return pltpu.make_async_remote_copy(
            src_ref=mine,
            dst_ref=sketches.at[here],
            send_sem=s_send.at[step - 1],
            recv_sem=s_recv.at[step - 1],
            device_id={"store": lax.rem(here + step, n_store), "sketch": core},
            device_id_type=MESH,
        )

    each(1, n_store, lambda i: sketch_copy(i).start())

    padded = parts.shape[0] * parts.shape[1]
    slot = lax.broadcasted_iota(jnp.int32, (padded, 1), 0)
    within = slot % parts.shape[1]
    label = jnp.where(within < share, slot // parts.shape[1] * share + within, -1)
    onehot = (label == rows_ref[...]).astype(jnp.bfloat16)
    loads[4].wait()
    ahead = sums_hi is not None
    if ahead:
        step = 256
        for at in range(0, store.shape[1], step):
            hi, lo = split(jnp.dot(onehot, store[:, at:at + step], preferred_element_type=jnp.float32))
            sums_hi[:, at:at + step] = hi
            sums_lo[:, at:at + step] = lo

    each(1, n_store, lambda i: sketch_copy(i).wait_recv())
    blocks = mine.shape[0]
    wide[...] = sketches[...].astype(jnp.float32).reshape(wide.shape)
    queries = jnp.concatenate(
        [wide[pl.ds(j, n_store, stride=blocks), :].astype(jnp.bfloat16) for j in range(blocks)], axis=1
    )
    dot = functools.partial(lax.dot_general, preferred_element_type=jnp.float32)
    if ahead:
        part = dot(sums_hi[...], queries, NT) + dot(sums_lo[...], queries, NT)
    else:
        hi, lo = split(dot(store[...], queries, NT))
        part = jnp.dot(onehot, hi, preferred_element_type=jnp.float32)
        part = part + jnp.dot(onehot, lo, preferred_element_type=jnp.float32)
    parts[:, :, :n_store] = part.reshape(parts.shape[0], parts.shape[1], n_store)

    def part_copy(step):
        to = lax.rem(me + step, n_all)
        return pltpu.make_async_remote_copy(
            src_ref=parts.at[to],
            dst_ref=landed.at[step - 1],
            send_sem=p_send.at[step - 1],
            recv_sem=p_recv.at[step - 1],
            device_id=peer(step),
            device_id_type=MESH,
        )

    each(1, n_all, lambda i: part_copy(i).start())
    each(1, n_all, lambda i: part_copy(i).wait_recv())
    total = parts[me] + jnp.sum(landed[...], axis=0)
    out_ref[...] = total[:share, :n_store]
    each(1, n_store, lambda i: sketch_copy(i).wait_send())
    each(1, n_all, lambda i: part_copy(i).wait_send())


def local(acts, grads, proj_in, proj_out, token_ids, store, row_example):
    n_store, n_sketch = lax.axis_size("store"), lax.axis_size("sketch")
    n_all = n_store * n_sketch
    depth, width = proj_in.shape[1:]
    tokens = acts.shape[1]
    assert tokens == SEQ
    rows = store.shape[0]
    share = rows // (16 * n_sketch)
    tall = -(-share // SUBLANES) * SUBLANES
    across = -(-n_store // LANES) * LANES
    blocks = width * width // LANES
    ahead = n_all * tall <= 256
    sums = pltpu.VMEM((n_all * tall, store.shape[1]), jnp.bfloat16) if ahead else None
    hbm = pl.BlockSpec(memory_space=pl.ANY)
    vmem = pl.BlockSpec(memory_space=pltpu.VMEM)
    return pl.pallas_call(
        functools.partial(kernel, n_store, n_sketch, share),
        out_shape=jax.ShapeDtypeStruct((share, n_store), jnp.float32),
        in_specs=[hbm, hbm, hbm, hbm, vmem, hbm, vmem],
        out_specs=vmem,
        scratch_shapes=[
            pltpu.VMEM((tokens, depth), jnp.bfloat16),
            pltpu.VMEM((tokens, depth), jnp.bfloat16),
            pltpu.VMEM((width, depth), jnp.bfloat16),
            pltpu.VMEM((width, depth), jnp.bfloat16),
            pltpu.VMEM(store.shape, jnp.bfloat16),
            pltpu.VMEM((width, width), jnp.float32),
            pltpu.VMEM((blocks, LANES), jnp.bfloat16),
            pltpu.VMEM((n_store, blocks, LANES), jnp.bfloat16),
            pltpu.VMEM((n_store * blocks, LANES), jnp.float32),
            sums,
            sums,
            pltpu.VMEM((n_all, tall, across), jnp.float32),
            pltpu.VMEM((n_all - 1, tall, across), jnp.float32),
            pltpu.SemaphoreType.DMA((5,)),
            pltpu.SemaphoreType.DMA((n_store - 1,)),
            pltpu.SemaphoreType.DMA((n_store - 1,)),
            pltpu.SemaphoreType.DMA((n_all - 1,)),
            pltpu.SemaphoreType.DMA((n_all - 1,)),
        ],
        compiler_params=pltpu.CompilerParams(
            collective_id=0, has_side_effects=True, vmem_limit_bytes=48 * 1024 * 1024
        ),
    )(
        acts[0], grads[0], proj_in[0].T, proj_out[0].T,
        token_ids.reshape(1, tokens), store, row_example.reshape(1, rows),
    )


def solution(mesh):
    in_specs = (
        P("sketch", ("group", "store"), None),
        P("sketch", ("group", "store"), None),
        P("sketch", None, None),
        P("sketch", None, None),
        P(("group", "store")),
        P(("group", "store"), "sketch"),
        P(("group", "store")),
    )
    out_specs = P(("group", "store", "sketch"), None)
    return jax.shard_map(local, mesh=mesh, in_specs=in_specs, out_specs=out_specs, check_vma=False)
```

time: 97.7 us -> 24.7 us (0.25)
  blocking collectives: 90 us -> 0 us
  Pallas kernels: 0 us -> 16.4 us
  local copies, waits for them, and re-layouts: 1.3 us -> 7.87 us
  matrix products: 4.05 us -> 0 us
  other arithmetic: 1.41 us -> 0 us
    unnamed x1 -> x0, blocking collectives: 57.7 us -> none
    all_gather x1 -> x0, blocking collectives: 32.3 us -> none  [local(): lax.all_gather(sketch, 'store', axis=0, tiled=True)]
    pallas_call x0 -> x1, Pallas kernels: none -> 16.4 us  [local(): pl.pallas_call(functools.partial(kernel, n_store, n_sketch, share), out_s...]
    unnamed x15, local copies, waits for them, and re-layouts: 1.3 us -> 7.87 us
    dot_general x5 -> x0, matrix products: 4.05 us -> none  [the longest x1 1.91 us: local(): jnp.dot(grads[0], proj_out[0], preferred_element_type=jnp.float32)]
where the time goes in v1:
time: 24.7 us; the launch traced here: 24.3 us
  Pallas kernels  16.4 us (66%)
  local copies, waits for them, and re-layouts  7.87 us (32%)
    pallas_call x1, Pallas kernels, local(): pl.pallas_call(functools.partial(kernel, n_store, n_sketch, share), out_s...  16.4 us
    unnamed x15, local copies, waits for them, and re-layouts  7.87 us

profile of v1, /device:TPU:0, one launch (start us, length us, event | category | flops | bytes accessed | tf_op | source)
XLA Modules:
  0.0 24.3 jit_solution(9239535877170199302)
XLA Ops:
  0.0 0.0 copy-start
  0.0 1.4 %copy-done = bf16[192,4096]{1,0:T(8,128)(2,1)S(1)} copy-done((bf16[192,4096]{1,0:T(8,128)(2,1)S(1)}, bf16[192,4096]{1,0:T(8,128)(2,1)}, u32[]{:S(2)}) %copy-start) | copy-done | bytes 1572888
  1.4 0.0 copy-start.1
  1.4 1.2 %copy-done.1 = bf16[1,128,4096]{2,1,0:T(8,128)(2,1)S(1)} copy-done((bf16[1,128,4096]{2,1,0:T(8,128)(2,1)S(1)}, bf16[1,128,4096]{2,1,0:T(8,128)(2,1)}, u32[]{:S(2)}) %copy-start.1) | copy-done | bytes 1048600
  2.6 0.0 copy-start.2
  2.6 1.2 %copy-done.2 = bf16[1,128,4096]{2,1,0:T(8,128)(2,1)S(1)} copy-done((bf16[1,128,4096]{2,1,0:T(8,128)(2,1)S(1)}, bf16[1,128,4096]{2,1,0:T(8,128)(2,1)}, u32[]{:S(2)}) %copy-start.2) | copy-done | bytes 1048600
  3.9 0.0 copy-start.3
  3.9 1.0 %copy-done.3 = bf16[1,4096,64]{1,2,0:T(8,128)(2,1)S(1)} copy-done((bf16[1,4096,64]{1,2,0:T(8,128)(2,1)S(1)}, bf16[1,4096,64]{1,2,0:T(8,128)(2,1)}, u32[]{:S(2)}) %copy-start.3) | copy-done | bytes 524312
  4.9 0.0 copy-start.4
  4.9 1.0 %copy-done.4 = bf16[1,4096,64]{1,2,0:T(8,128)(2,1)S(1)} copy-done((bf16[1,4096,64]{1,2,0:T(8,128)(2,1)S(1)}, bf16[1,4096,64]{1,2,0:T(8,128)(2,1)}, u32[]{:S(2)}) %copy-start.4) | copy-done | bytes 524312
  5.9 0.0 copy-start.5
  5.9 0.7 %copy-done.5 = s32[192]{0:T(256)S(1)} copy-done((s32[192]{0:T(256)S(1)}, s32[192]{0:T(256)}, u32[]{:S(2)}) %copy-start.5) | copy-done | bytes 792
  6.6 0.0 copy-start.6
  6.6 0.7 %copy-done.6 = s32[128]{0:T(128)S(1)} copy-done((s32[128]{0:T(128)S(1)}, s32[128]{0:T(128)}, u32[]{:S(2)}) %copy-start.6) | copy-done | bytes 536
  7.3 16.4 %shard_map.73 = f32[6,8]{1,0:T(8,128)S(1)} custom-call(bf16[128,4096]{1,0:T(8,128)(2,1)S(1)} %bitcast.10, bf16[128,4096]{1,0:T(8,128)(2,1)S(1)} %bitcast.11, bf16[64,4096]{1,0:T(8,128)(2,1)S(1)} %bitcast.12, bf16[64,4096]{1,0:T(8,128)(2,1)S(1)} %bitcast.13, s32[1,128]{1,0:T(1,128)S(1)} %bitcast.15, bf16[192,4096]{1,0:T(8,128)(2,1)S(1)} %copy-done, ...), custom_call_target="tpu_custom_call" | custom-call | tf_op jit(solution)/shard_map/pallas_call | solution.py:161
  23.7 0.6 %copy.9 = f32[6,8]{1,0:T(8,128)} copy(f32[6,8]{1,0:T(8,128)S(1)} %shard_map.73) | data formatting | bytes 384
Async XLA Ops:
  0.0 1.4 %copy-start = (bf16[192,4096]{1,0:T(8,128)(2,1)S(1)}, bf16[192,4096]{1,0:T(8,128)(2,1)}, u32[]{:S(2)}) copy-start(bf16[192,4096]{1,0:T(8,128)(2,1)} %store_hbm.1) | copy-start | bytes 4718596
  1.4 1.2 %copy-start.1 = (bf16[1,128,4096]{2,1,0:T(8,128)(2,1)S(1)}, bf16[1,128,4096]{2,1,0:T(8,128)(2,1)}, u32[]{:S(2)}) copy-start(bf16[1,128,4096]{2,1,0:T(8,128)(2,1)} %param.7) | copy-start | bytes 3145732
  2.6 1.2 %copy-start.2 = (bf16[1,128,4096]{2,1,0:T(8,128)(2,1)S(1)}, bf16[1,128,4096]{2,1,0:T(8,128)(2,1)}, u32[]{:S(2)}) copy-start(bf16[1,128,4096]{2,1,0:T(8,128)(2,1)} %param.8) | copy-start | bytes 3145732
  3.9 1.0 %copy-start.3 = (bf16[1,4096,64]{1,2,0:T(8,128)(2,1)S(1)}, bf16[1,4096,64]{1,2,0:T(8,128)(2,1)}, u32[]{:S(2)}) copy-start(bf16[1,4096,64]{1,2,0:T(8,128)(2,1)} %param.9) | copy-start | bytes 1572868
  4.9 1.0 %copy-start.4 = (bf16[1,4096,64]{1,2,0:T(8,128)(2,1)S(1)}, bf16[1,4096,64]{1,2,0:T(8,128)(2,1)}, u32[]{:S(2)}) copy-start(bf16[1,4096,64]{1,2,0:T(8,128)(2,1)} %param.10) | copy-start | bytes 1572868
  5.9 0.7 %copy-start.5 = (s32[192]{0:T(256)S(1)}, s32[192]{0:T(256)}, u32[]{:S(2)}) copy-start(s32[192]{0:T(256)} %param.13) | copy-start | bytes 2308
  6.6 0.7 %copy-start.6 = (s32[128]{0:T(128)S(1)}, s32[128]{0:T(128)}, u32[]{:S(2)}) copy-start(s32[128]{0:T(128)} %param.11) | copy-start | bytes 1540

commit v2 on v1

--- a/solution.py
+++ b/solution.py
@@ -30,15 +30,18 @@
 
 def kernel(
     n_store, n_sketch, share,
-    acts_hbm, grads_hbm, pin_hbm, pout_hbm, ids_ref, store_hbm, rows_ref,
+    acts_hbm, grads_hbm, pin_hbm, pout_hbm, ids_hbm, store_hbm, rows_hbm,
     out_ref,
-    acts, grads, pin, pout, store, outer_ref, mine, sketches, wide, sums_hi, sums_lo, parts, landed,
+    acts, grads, pin, pout, store, ids_ref, rows_ref, outer_ref, mine, sketches, wide, sums_hi, sums_lo, parts, landed,
     load_sem, s_send, s_recv, p_send, p_recv,
 ):
     loads = [
         pltpu.make_async_copy(src, dst, load_sem.at[i])
         for i, (src, dst) in enumerate(
-            ((pout_hbm, pout), (grads_hbm, grads), (pin_hbm, pin), (acts_hbm, acts), (store_hbm, store))
+            (
+                (ids_hbm, ids_ref), (pout_hbm, pout), (grads_hbm, grads), (pin_hbm, pin), (acts_hbm, acts),
+                (rows_hbm, rows_ref), (store_hbm, store),
+            )
         )
     ]
     for load in loads:
@@ -57,13 +60,14 @@
     each(1, n_all, lambda i: pl.semaphore_signal(barrier, 1, device_id=peer(i), device_id_type=MESH))
 
     width = pout.shape[0]
+    loads[0].wait()
     keep = (ids_ref[...] != PAD_ID).astype(jnp.float32)
     count = jnp.sum(keep, axis=1, keepdims=True)
-    loads[0].wait()
     loads[1].wait()
+    loads[2].wait()
     gp = lax.dot_general(pout[...], grads[...], NT, preferred_element_type=jnp.float32) * keep
-    loads[2].wait()
     loads[3].wait()
+    loads[4].wait()
     xp = lax.dot_general(pin[...], acts[...], NT, preferred_element_type=jnp.float32)
     g_hi, g_lo = split(gp)
     x_hi, x_lo = split(xp)
@@ -99,8 +103,9 @@
     slot = lax.broadcasted_iota(jnp.int32, (padded, 1), 0)
     within = slot % parts.shape[1]
     label = jnp.where(within < share, slot // parts.shape[1] * share + within, -1)
+    loads[5].wait()
     onehot = (label == rows_ref[...]).astype(jnp.bfloat16)
-    loads[4].wait()
+    loads[6].wait()
     ahead = sums_hi is not None
     if ahead:
         step = 256
@@ -156,12 +161,12 @@
     blocks = width * width // LANES
     ahead = n_all * tall <= 256
     sums = pltpu.VMEM((n_all * tall, store.shape[1]), jnp.bfloat16) if ahead else None
-    hbm = pl.BlockSpec(memory_space=pl.ANY)
+    hbm = pl.BlockSpec(memory_space=pltpu.HBM)
     vmem = pl.BlockSpec(memory_space=pltpu.VMEM)
     return pl.pallas_call(
         functools.partial(kernel, n_store, n_sketch, share),
         out_shape=jax.ShapeDtypeStruct((share, n_store), jnp.float32),
-        in_specs=[hbm, hbm, hbm, hbm, vmem, hbm, vmem],
+        in_specs=[hbm] * 7,
         out_specs=vmem,
         scratch_shapes=[
             pltpu.VMEM((tokens, depth), jnp.bfloat16),
@@ -169,6 +174,8 @@
             pltpu.VMEM((width, depth), jnp.bfloat16),
             pltpu.VMEM((width, depth), jnp.bfloat16),
             pltpu.VMEM(store.shape, jnp.bfloat16),
+            pltpu.VMEM((1, tokens), jnp.int32),
+            pltpu.VMEM((1, rows), jnp.int32),
             pltpu.VMEM((width, width), jnp.float32),
             pltpu.VMEM((blocks, LANES), jnp.bfloat16),
             pltpu.VMEM((n_store, blocks, LANES), jnp.bfloat16),
@@ -177,14 +184,14 @@
             sums,
             pltpu.VMEM((n_all, tall, across), jnp.float32),
             pltpu.VMEM((n_all - 1, tall, across), jnp.float32),
-            pltpu.SemaphoreType.DMA((5,)),
+            pltpu.SemaphoreType.DMA((7,)),
             pltpu.SemaphoreType.DMA((n_store - 1,)),
             pltpu.SemaphoreType.DMA((n_store - 1,)),
             pltpu.SemaphoreType.DMA((n_all - 1,)),
             pltpu.SemaphoreType.DMA((n_all - 1,)),
         ],
         compiler_params=pltpu.CompilerParams(
-            collective_id=0, has_side_effects=True, vmem_limit_bytes=48 * 1024 * 1024
+            collective_id=0, has_side_effects=True, vmem_limit_bytes=63 * 1024 * 1024
         ),
     )(
         acts[0], grads[0], proj_in[0].T, proj_out[0].T,

time: 24.7 us -> 18.2 us (0.74)
  local copies, waits for them, and re-layouts: 7.87 us -> 1.28 us
  Pallas kernels: 16.4 us -> 16.7 us
    unnamed x15 -> x1, local copies, waits for them, and re-layouts: 7.87 us -> 1.28 us
    pallas_call x1, Pallas kernels: 16.4 us -> 16.7 us  [local(): pl.pallas_call(functools.partial(kernel, n_store, n_sketch, share), out_s...]
where the time goes in v2:
time: 18.2 us; the launch traced here: 18 us
  Pallas kernels  16.7 us (92%)
  local copies, waits for them, and re-layouts  1.28 us (7%)
    pallas_call x1, Pallas kernels, local(): pl.pallas_call(functools.partial(kernel, n_store, n_sketch, share), out_s...  16.7 us
    unnamed x1, local copies, waits for them, and re-layouts  1.28 us

profile of v2, /device:TPU:0, one launch (start us, length us, event | category | flops | bytes accessed | tf_op | source)
XLA Modules:
  0.0 18.0 jit_solution(1430661640786524291)
XLA Ops:
  0.0 16.7 %shard_map.73 = f32[6,8]{1,0:T(8,128)} custom-call(bf16[128,4096]{1,0:T(8,128)(2,1)} %bitcast.10, bf16[128,4096]{1,0:T(8,128)(2,1)} %bitcast.11, bf16[64,4096]{1,0:T(8,128)(2,1)} %bitcast.12, bf16[64,4096]{1,0:T(8,128)(2,1)} %bitcast.13, s32[1,128]{1,0:T(1,128)} %bitcast.15, bf16[192,4096]{1,0:T(8,128)(2,1)} %store_hbm.1, s32[1,192]{1,0:T(1,128)} %bitcast.14), custom_call_target="tpu_custom_call" | custom-call | tf_op jit(solution)/shard_map/pallas_call | solution.py:166
  16.7 1.3 %copy.9 = f32[6,8]{1,0:T(8,128)} copy(f32[6,8]{1,0:T(8,128)} %shard_map.73) | data formatting | bytes 384

commit v3 on v2

--- a/solution.py
+++ b/solution.py
@@ -10,7 +10,6 @@
 SEQ = 128
 PAD_ID = 128004
 LANES = 128
-SUBLANES = 8
 NT = (((1,), (1,)), ((), ()))
 MESH = pl.DeviceIdType.MESH
 
@@ -44,7 +43,7 @@
             )
         )
     ]
-    for load in loads:
+    for load in loads[:-1]:
         load.start()
 
     here = lax.axis_index("store")
@@ -68,6 +67,7 @@
     gp = lax.dot_general(pout[...], grads[...], NT, preferred_element_type=jnp.float32) * keep
     loads[3].wait()
     loads[4].wait()
+    loads[6].start()
     xp = lax.dot_general(pin[...], acts[...], NT, preferred_element_type=jnp.float32)
     g_hi, g_lo = split(gp)
     x_hi, x_lo = split(xp)
@@ -99,10 +99,8 @@
 
     each(1, n_store, lambda i: sketch_copy(i).start())
 
-    padded = parts.shape[0] * parts.shape[1]
-    slot = lax.broadcasted_iota(jnp.int32, (padded, 1), 0)
-    within = slot % parts.shape[1]
-    label = jnp.where(within < share, slot // parts.shape[1] * share + within, -1)
+    slot = lax.broadcasted_iota(jnp.int32, (n_all * share, 1), 0)
+    label = slot % n_all * share + slot // n_all
     loads[5].wait()
     onehot = (label == rows_ref[...]).astype(jnp.bfloat16)
     loads[6].wait()
@@ -127,7 +125,10 @@
         hi, lo = split(dot(store[...], queries, NT))
         part = jnp.dot(onehot, hi, preferred_element_type=jnp.float32)
         part = part + jnp.dot(onehot, lo, preferred_element_type=jnp.float32)
-    parts[:, :, :n_store] = part.reshape(parts.shape[0], parts.shape[1], n_store)
+    packed = jnp.concatenate([part[j * n_all:(j + 1) * n_all] for j in range(share)], axis=1)
+    if parts.shape[2] > packed.shape[1]:
+        packed = jnp.pad(packed, ((0, 0), (0, parts.shape[2] - packed.shape[1])))
+    parts[...] = packed.reshape(parts.shape)
 
     def part_copy(step):
         to = lax.rem(me + step, n_all)
@@ -143,7 +144,9 @@
     each(1, n_all, lambda i: part_copy(i).start())
     each(1, n_all, lambda i: part_copy(i).wait_recv())
     total = parts[me] + jnp.sum(landed[...], axis=0)
-    out_ref[...] = total[:share, :n_store]
+    out_ref[...] = jnp.concatenate(
+        [total[:, j * n_store:(j + 1) * n_store] for j in range(share)], axis=0
+    )
     each(1, n_store, lambda i: sketch_copy(i).wait_send())
     each(1, n_all, lambda i: part_copy(i).wait_send())
 
@@ -156,11 +159,10 @@
     assert tokens == SEQ
     rows = store.shape[0]
     share = rows // (16 * n_sketch)
-    tall = -(-share // SUBLANES) * SUBLANES
-    across = -(-n_store // LANES) * LANES
+    across = -(-share * n_store // LANES) * LANES
     blocks = width * width // LANES
-    ahead = n_all * tall <= 256
-    sums = pltpu.VMEM((n_all * tall, store.shape[1]), jnp.bfloat16) if ahead else None
+    ahead = n_all * share <= 256
+    sums = pltpu.VMEM((n_all * share, store.shape[1]), jnp.bfloat16) if ahead else None
     hbm = pl.BlockSpec(memory_space=pltpu.HBM)
     vmem = pl.BlockSpec(memory_space=pltpu.VMEM)
     return pl.pallas_call(
@@ -182,8 +184,8 @@
             pltpu.VMEM((n_store * blocks, LANES), jnp.float32),
             sums,
             sums,
-            pltpu.VMEM((n_all, tall, across), jnp.float32),
-            pltpu.VMEM((n_all - 1, tall, across), jnp.float32),
+            pltpu.VMEM((n_all, 1, across), jnp.float32),
+            pltpu.VMEM((n_all - 1, 1, across), jnp.float32),
             pltpu.SemaphoreType.DMA((7,)),
             pltpu.SemaphoreType.DMA((n_store - 1,)),
             pltpu.SemaphoreType.DMA((n_store - 1,)),

time: 18.2 us -> 18 us (0.989)
  Pallas kernels: 16.7 us -> 16.5 us
    pallas_call x1, Pallas kernels: 16.7 us -> 16.5 us  [local(): pl.pallas_call(functools.partial(kernel, n_store, n_sketch, share), out_s...]
where the time goes in v3:
time: 18 us; the launch traced here: 17.8 us
  Pallas kernels  16.5 us (92%)
  local copies, waits for them, and re-layouts  1.28 us (7%)
    pallas_call x1, Pallas kernels, local(): pl.pallas_call(functools.partial(kernel, n_store, n_sketch, share), out_s...  16.5 us
    unnamed x1, local copies, waits for them, and re-layouts  1.28 us

profile of v3, /device:TPU:0, one launch (start us, length us, event | category | flops | bytes accessed | tf_op | source)
XLA Modules:
  0.0 17.8 jit_solution(13410402171618253190)
XLA Ops:
  0.0 16.5 %shard_map.73 = f32[6,8]{1,0:T(8,128)} custom-call(bf16[128,4096]{1,0:T(8,128)(2,1)} %bitcast.10, bf16[128,4096]{1,0:T(8,128)(2,1)} %bitcast.11, bf16[64,4096]{1,0:T(8,128)(2,1)} %bitcast.12, bf16[64,4096]{1,0:T(8,128)(2,1)} %bitcast.13, s32[1,128]{1,0:T(1,128)} %bitcast.15, bf16[192,4096]{1,0:T(8,128)(2,1)} %store_hbm.1, s32[1,192]{1,0:T(1,128)} %bitcast.14), custom_call_target="tpu_custom_call" | custom-call | tf_op jit(solution)/shard_map/pallas_call | solution.py:168
  16.5 1.3 %copy.9 = f32[6,8]{1,0:T(8,128)} copy(f32[6,8]{1,0:T(8,128)} %shard_map.73) | data formatting | bytes 384

commit v4 on v3

--- a/solution.py
+++ b/solution.py
@@ -52,8 +52,7 @@
     me = here * n_sketch + core
 
     def peer(step):
-        to = lax.rem(me + step, n_all)
-        return {"store": to // n_sketch, "sketch": lax.rem(to, n_sketch)}
+        return {"store": here ^ (step // n_sketch), "sketch": core ^ (step % n_sketch)}
 
     barrier = pltpu.get_barrier_semaphore()
     each(1, n_all, lambda i: pl.semaphore_signal(barrier, 1, device_id=peer(i), device_id_type=MESH))
@@ -91,9 +90,9 @@
         return pltpu.make_async_remote_copy(
             src_ref=mine,
             dst_ref=sketches.at[here],
-            send_sem=s_send.at[step - 1],
-            recv_sem=s_recv.at[step - 1],
-            device_id={"store": lax.rem(here + step, n_store), "sketch": core},
+            send_sem=s_send,
+            recv_sem=s_recv,
+            device_id={"store": here ^ step, "sketch": core},
             device_id_type=MESH,
         )
 
@@ -112,7 +111,8 @@
             sums_hi[:, at:at + step] = hi
             sums_lo[:, at:at + step] = lo
 
-    each(1, n_store, lambda i: sketch_copy(i).wait_recv())
+    others = sketches.at[pl.ds(1, n_store - 1)]
+    pltpu.make_async_copy(others, others, s_recv).wait()
     blocks = mine.shape[0]
     wide[...] = sketches[...].astype(jnp.float32).reshape(wide.shape)
     queries = jnp.concatenate(
@@ -131,24 +131,23 @@
     parts[...] = packed.reshape(parts.shape)
 
     def part_copy(step):
-        to = lax.rem(me + step, n_all)
         return pltpu.make_async_remote_copy(
-            src_ref=parts.at[to],
+            src_ref=parts.at[me ^ step],
             dst_ref=landed.at[step - 1],
-            send_sem=p_send.at[step - 1],
-            recv_sem=p_recv.at[step - 1],
+            send_sem=p_send,
+            recv_sem=p_recv,
             device_id=peer(step),
             device_id_type=MESH,
         )
 
     each(1, n_all, lambda i: part_copy(i).start())
-    each(1, n_all, lambda i: part_copy(i).wait_recv())
+    pltpu.make_async_copy(landed, landed, p_recv).wait()
     total = parts[me] + jnp.sum(landed[...], axis=0)
     out_ref[...] = jnp.concatenate(
         [total[:, j * n_store:(j + 1) * n_store] for j in range(share)], axis=0
     )
-    each(1, n_store, lambda i: sketch_copy(i).wait_send())
-    each(1, n_all, lambda i: part_copy(i).wait_send())
+    pltpu.make_async_copy(others, others, s_send).wait()
+    pltpu.make_async_copy(landed, landed, p_send).wait()
 
 
 def local(acts, grads, proj_in, proj_out, token_ids, store, row_example):
@@ -156,7 +155,7 @@
     n_all = n_store * n_sketch
     depth, width = proj_in.shape[1:]
     tokens = acts.shape[1]
-    assert tokens == SEQ
+    assert tokens == SEQ and n_all & (n_all - 1) == 0
     rows = store.shape[0]
     share = rows // (16 * n_sketch)
     across = -(-share * n_store // LANES) * LANES
@@ -187,10 +186,10 @@
             pltpu.VMEM((n_all, 1, across), jnp.float32),
             pltpu.VMEM((n_all - 1, 1, across), jnp.float32),
             pltpu.SemaphoreType.DMA((7,)),
-            pltpu.SemaphoreType.DMA((n_store - 1,)),
-            pltpu.SemaphoreType.DMA((n_store - 1,)),
-            pltpu.SemaphoreType.DMA((n_all - 1,)),
-            pltpu.SemaphoreType.DMA((n_all - 1,)),
+            pltpu.SemaphoreType.DMA,
+            pltpu.SemaphoreType.DMA,
+            pltpu.SemaphoreType.DMA,
+            pltpu.SemaphoreType.DMA,
         ],
         compiler_params=pltpu.CompilerParams(
             collective_id=0, has_side_effects=True, vmem_limit_bytes=63 * 1024 * 1024

time: 18 us -> 17.7 us (0.983)
  Pallas kernels: 16.5 us -> 16.3 us
    pallas_call x1, Pallas kernels: 16.5 us -> 16.3 us  [local(): pl.pallas_call(functools.partial(kernel, n_store, n_sketch, share), out_s...]
where the time goes in v4:
time: 17.7 us; the launch traced here: 17.5 us
  Pallas kernels  16.3 us (92%)
  local copies, waits for them, and re-layouts  1.28 us (7%)
    pallas_call x1, Pallas kernels, local(): pl.pallas_call(functools.partial(kernel, n_store, n_sketch, share), out_s...  16.3 us
    unnamed x1, local copies, waits for them, and re-layouts  1.28 us

profile of v4, /device:TPU:0, one launch (start us, length us, event | category | flops | bytes accessed | tf_op | source)
XLA Modules:
  0.0 17.5 jit_solution(277646091053868897)
XLA Ops:
  0.0 16.3 %shard_map.73 = f32[6,8]{1,0:T(8,128)} custom-call(bf16[128,4096]{1,0:T(8,128)(2,1)} %bitcast.10, bf16[128,4096]{1,0:T(8,128)(2,1)} %bitcast.11, bf16[64,4096]{1,0:T(8,128)(2,1)} %bitcast.12, bf16[64,4096]{1,0:T(8,128)(2,1)} %bitcast.13, s32[1,128]{1,0:T(1,128)} %bitcast.15, bf16[192,4096]{1,0:T(8,128)(2,1)} %store_hbm.1, s32[1,192]{1,0:T(1,128)} %bitcast.14), custom_call_target="tpu_custom_call" | custom-call | tf_op jit(solution)/shard_map/pallas_call | solution.py:167
  16.3 1.3 %copy.9 = f32[6,8]{1,0:T(8,128)} copy(f32[6,8]{1,0:T(8,128)} %shard_map.73) | data formatting | bytes 384

commit v5 on v4

--- a/solution.py
+++ b/solution.py
@@ -14,12 +14,12 @@
 MESH = pl.DeviceIdType.MESH
 
 
-def each(start, stop, body):
-    if stop - start <= 16:
-        for i in range(start, stop):
+def each(count, body):
+    if count <= 16:
+        for i in reversed(range(1, count)):
             body(i)
     else:
-        lax.fori_loop(start, stop, lambda i, carry: (body(i), carry)[1], 0)
+        lax.fori_loop(1, count, lambda i, carry: (body(count - i), carry)[1], 0)
 
 
 def split(value):
@@ -31,7 +31,7 @@
     n_store, n_sketch, share,
     acts_hbm, grads_hbm, pin_hbm, pout_hbm, ids_hbm, store_hbm, rows_hbm,
     out_ref,
-    acts, grads, pin, pout, store, ids_ref, rows_ref, outer_ref, mine, sketches, wide, sums_hi, sums_lo, parts, landed,
+    acts, grads, pin, pout, store, ids_ref, rows_ref, outer_ref, mine, sketches, wide, sums, parts, landed,
     load_sem, s_send, s_recv, p_send, p_recv,
 ):
     loads = [
@@ -55,7 +55,7 @@
         return {"store": here ^ (step // n_sketch), "sketch": core ^ (step % n_sketch)}
 
     barrier = pltpu.get_barrier_semaphore()
-    each(1, n_all, lambda i: pl.semaphore_signal(barrier, 1, device_id=peer(i), device_id_type=MESH))
+    each(n_all, lambda i: pl.semaphore_signal(barrier, 1, device_id=peer(i), device_id_type=MESH))
 
     width = pout.shape[0]
     loads[0].wait()
@@ -96,20 +96,20 @@
             device_id_type=MESH,
         )
 
-    each(1, n_store, lambda i: sketch_copy(i).start())
+    each(n_store, lambda i: sketch_copy(i).start())
 
     slot = lax.broadcasted_iota(jnp.int32, (n_all * share, 1), 0)
     label = slot % n_all * share + slot // n_all
     loads[5].wait()
     onehot = (label == rows_ref[...]).astype(jnp.bfloat16)
     loads[6].wait()
-    ahead = sums_hi is not None
+    ahead = sums is not None
     if ahead:
         step = 256
         for at in range(0, store.shape[1], step):
             hi, lo = split(jnp.dot(onehot, store[:, at:at + step], preferred_element_type=jnp.float32))
-            sums_hi[:, at:at + step] = hi
-            sums_lo[:, at:at + step] = lo
+            sums[:n_all * share, at:at + step] = hi
+            sums[n_all * share:, at:at + step] = lo
 
     others = sketches.at[pl.ds(1, n_store - 1)]
     pltpu.make_async_copy(others, others, s_recv).wait()
@@ -120,7 +120,8 @@
     )
     dot = functools.partial(lax.dot_general, preferred_element_type=jnp.float32)
     if ahead:
-        part = dot(sums_hi[...], queries, NT) + dot(sums_lo[...], queries, NT)
+        both = dot(sums[...], queries, NT)
+        part = both[:n_all * share] + both[n_all * share:]
     else:
         hi, lo = split(dot(store[...], queries, NT))
         part = jnp.dot(onehot, hi, preferred_element_type=jnp.float32)
@@ -140,7 +141,7 @@
             device_id_type=MESH,
         )
 
-    each(1, n_all, lambda i: part_copy(i).start())
+    each(n_all, lambda i: part_copy(i).start())
     pltpu.make_async_copy(landed, landed, p_recv).wait()
     total = parts[me] + jnp.sum(landed[...], axis=0)
     out_ref[...] = jnp.concatenate(
@@ -161,7 +162,7 @@
     across = -(-share * n_store // LANES) * LANES
     blocks = width * width // LANES
     ahead = n_all * share <= 256
-    sums = pltpu.VMEM((n_all * share, store.shape[1]), jnp.bfloat16) if ahead else None
+    sums = pltpu.VMEM((2 * n_all * share, store.shape[1]), jnp.bfloat16) if ahead else None
     hbm = pl.BlockSpec(memory_space=pltpu.HBM)
     vmem = pl.BlockSpec(memory_space=pltpu.VMEM)
     return pl.pallas_call(
@@ -182,7 +183,6 @@
             pltpu.VMEM((n_store, blocks, LANES), jnp.bfloat16),
             pltpu.VMEM((n_store * blocks, LANES), jnp.float32),
             sums,
-            sums,
             pltpu.VMEM((n_all, 1, across), jnp.float32),
             pltpu.VMEM((n_all - 1, 1, across), jnp.float32),
             pltpu.SemaphoreType.DMA((7,)),

time: 17.7 us -> 16.8 us (0.949)
  Pallas kernels: 16.3 us -> 15.3 us
    pallas_call x1, Pallas kernels: 16.3 us -> 15.3 us  [local(): pl.pallas_call(functools.partial(kernel, n_store, n_sketch, share), out_s...]
where the time goes in v5:
time: 16.8 us; the launch traced here: 16.6 us
  Pallas kernels  15.3 us (91%)
  local copies, waits for them, and re-layouts  1.28 us (8%)
    pallas_call x1, Pallas kernels, local(): pl.pallas_call(functools.partial(kernel, n_store, n_sketch, share), out_s...  15.3 us
    unnamed x1, local copies, waits for them, and re-layouts  1.28 us

profile of v5, /device:TPU:0, one launch (start us, length us, event | category | flops | bytes accessed | tf_op | source)
XLA Modules:
  0.0 16.6 jit_solution(14511044315024604561)
XLA Ops:
  0.0 15.3 %shard_map.73 = f32[6,8]{1,0:T(8,128)} custom-call(bf16[128,4096]{1,0:T(8,128)(2,1)} %bitcast.10, bf16[128,4096]{1,0:T(8,128)(2,1)} %bitcast.11, bf16[64,4096]{1,0:T(8,128)(2,1)} %bitcast.12, bf16[64,4096]{1,0:T(8,128)(2,1)} %bitcast.13, s32[1,128]{1,0:T(1,128)} %bitcast.15, bf16[192,4096]{1,0:T(8,128)(2,1)} %store_hbm.1, s32[1,192]{1,0:T(1,128)} %bitcast.14), custom_call_target="tpu_custom_call" | custom-call | tf_op jit(solution)/shard_map/pallas_call | solution.py:168
  15.3 1.3 %copy.9 = f32[6,8]{1,0:T(8,128)} copy(f32[6,8]{1,0:T(8,128)} %shard_map.73) | data formatting | bytes 384

commit v6 on v5

--- a/solution.py
+++ b/solution.py
@@ -144,7 +144,7 @@
     each(n_all, lambda i: part_copy(i).start())
     pltpu.make_async_copy(landed, landed, p_recv).wait()
     total = parts[me] + jnp.sum(landed[...], axis=0)
-    out_ref[...] = jnp.concatenate(
+    out_ref[:share] = jnp.concatenate(
         [total[:, j * n_store:(j + 1) * n_store] for j in range(share)], axis=0
     )
     pltpu.make_async_copy(others, others, s_send).wait()
@@ -167,7 +167,7 @@
     vmem = pl.BlockSpec(memory_space=pltpu.VMEM)
     return pl.pallas_call(
         functools.partial(kernel, n_store, n_sketch, share),
-        out_shape=jax.ShapeDtypeStruct((share, n_store), jnp.float32),
+        out_shape=jax.ShapeDtypeStruct((share // 8 * 8 + 8, n_store), jnp.float32),
         in_specs=[hbm] * 7,
         out_specs=vmem,
         scratch_shapes=[
@@ -197,7 +197,7 @@
     )(
         acts[0], grads[0], proj_in[0].T, proj_out[0].T,
         token_ids.reshape(1, tokens), store, row_example.reshape(1, rows),
-    )
+    )[:share]
 
 
 def solution(mesh):

time: 16.8 us -> 16.8 us (level)
  no operation moved by 1% of the time
where the time goes in v6:
time: 16.8 us; the launch traced here: 16.6 us
  Pallas kernels  15.3 us (91%)
  local copies, waits for them, and re-layouts  1.28 us (8%)
    pallas_call x1, Pallas kernels, local(): pl.pallas_call(functools.partial(kernel, n_store, n_sketch, share), out_s...  15.3 us
    unnamed x1, local copies, waits for them, and re-layouts  1.28 us

profile of v6, /device:TPU:0, one launch (start us, length us, event | category | flops | bytes accessed | tf_op | source)
XLA Modules:
  0.0 16.6 jit_solution(15463523207935670175)
XLA Ops:
  0.0 15.3 %shard_map.73 = f32[8,8]{1,0:T(8,128)} custom-call(bf16[128,4096]{1,0:T(8,128)(2,1)} %bitcast.11, bf16[128,4096]{1,0:T(8,128)(2,1)} %bitcast.12, bf16[64,4096]{1,0:T(8,128)(2,1)} %bitcast.13, bf16[64,4096]{1,0:T(8,128)(2,1)} %bitcast.14, s32[1,128]{1,0:T(1,128)} %bitcast.17, bf16[192,4096]{1,0:T(8,128)(2,1)} %store_hbm.1, s32[1,192]{1,0:T(1,128)} %bitcast.16), custom_call_target="tpu_custom_call" | custom-call | tf_op jit(solution)/shard_map/pallas_call | solution.py:168
  15.3 1.3 %copy.9 = f32[6,8]{1,0:T(8,128)} copy(f32[6,8]{1,0:T(8,128)} %bitcast.15) | data formatting | bytes 384
